TPU v7x, 512 devices: a whole 4x8x8 slice. The times are simulated.
512 devices in a mesh: vocab: 16 (over y, core), docs: 32 (over x, z).
Axes of the slice: x: 4, y: 8, z: 8, core: 2. Of those that a mesh axis runs over, the one named last changes fastest.
Arguments:
- counts: bfloat16 [65536, 4, 128], P(('vocab', 'docs')), may hold values from 0 to 2
- doc_owner: int32 [65536, 4], P(('vocab', 'docs')), may hold values from 0 to 511, all different within a row; in each aligned block of 128 rows (0 to 127, 128 to 255, ...) at most 2 rows name the same one
- doc_sub: int32 [65536, 4], P(('vocab', 'docs')), may hold values from 0 to 7
- doc_len: int32 [65536], P(('vocab', 'docs')), may hold values from 256 to 1023
- first_weight: bfloat16 [524288, 2048], P(('vocab', 'docs')), may hold values from -0.25 to 0.25
- first_bias: float32 [2048], replicated, may hold values from -3 to 3
- head_weight: bfloat16 [2048, 1536], P('vocab', 'docs'), may hold values from -0.125 to 0.125
- head_bias: float32 [1536], replicated, may hold values from -4 to 4
- factor: bfloat16 [1536, 1536], P('vocab', 'docs'), as said below
- noise_draw: bfloat16 [65536, 1536], P(('vocab', 'docs')), may hold values from -5 to 5
Outputs:
- sample: bfloat16 [65536, 1536], P(('vocab', 'docs'))
Inputs may be any that keep to these rules, and one draw needn't show every extreme that they name: `doc_owner`: each document names 4 different owners. The documents of one device name one owner in at most 2 slots, and on some device some owner is named in exactly 2 slots. `factor`: lower triangular; diagonal entries lie between 0.5 and 1.5.
All inputs are finite; a program needn't handle non-finite values.
Results may differ from a plain program's by a relative error of at most 0.0038.
Values may be sent and summed in bfloat16 or wider, within the bound.
No kernel may reach another device: no remote copies, remote signals or barrier semaphores. Data moves between devices by JAX's collectives and lax.ppermute only.
A program may use at most 128 MiB of HBM per device.

v0:
```python
import jax
import jax.numpy as jnp
from jax import lax
from jax.sharding import PartitionSpec as P


def local(
    counts,
    doc_owner,
    doc_sub,
    doc_len,
    first_weight,
    first_bias,
    head_weight,
    head_bias,
    factor,
    noise_draw,
):
    vocab_devices = lax.axis_size("vocab")
    docs_devices = lax.axis_size("docs")
    device_count = vocab_devices * docs_devices
    docs_here, slot_count, block_width = counts.shape
    hidden_width = first_weight.shape[1]
    per_owner = first_weight.shape[0] // block_width
    capacity = max(2, 2 * docs_here * slot_count // device_count)
    owner_flat = doc_owner.reshape(-1)
    onehot = (owner_flat[:, None] == jnp.arange(device_count, dtype=jnp.int32)[None, :]).astype(
        jnp.int32
    )
    position = jnp.sum(jnp.cumsum(onehot, axis=0) * onehot, axis=1) - 1
    slot_index = owner_flat * capacity + position
    flat_rows = counts.reshape(-1, block_width)
    send_rows = (
        jnp.zeros((device_count * capacity, block_width), counts.dtype)
        .at[slot_index]
        .set(flat_rows)
    )
    send_sub = (
        jnp.zeros((device_count * capacity,), jnp.bfloat16)
        .at[slot_index]
        .set(doc_sub.reshape(-1).astype(jnp.bfloat16))
    )
    send_rows = send_rows.reshape(vocab_devices, docs_devices, capacity, block_width)
    send_sub = send_sub.reshape(vocab_devices, docs_devices, capacity)
    got_rows, got_sub = (
        lax.all_to_all(
            lax.all_to_all(send_rows, "vocab", split_axis=0, concat_axis=0, tiled=True),
            "docs",
            split_axis=1,
            concat_axis=1,
            tiled=True,
        ),
        lax.all_to_all(
            lax.all_to_all(send_sub, "vocab", split_axis=0, concat_axis=0, tiled=True),
            "docs",
            split_axis=1,
            concat_axis=1,
            tiled=True,
        ),
    )
    got_rows = got_rows.reshape(-1, block_width)
    got_sub = got_sub.reshape(-1).astype(jnp.int32)
    select = (got_sub[:, None] == jnp.arange(per_owner, dtype=jnp.int32)[None, :]).astype(
        jnp.bfloat16
    )
    spread = (select[:, :, None] * got_rows[:, None, :]).reshape(-1, per_owner * block_width)
    owner_terms = jnp.dot(spread, first_weight, preferred_element_type=jnp.float32).astype(
        jnp.bfloat16
    )
    owner_terms = owner_terms.reshape(vocab_devices, docs_devices, capacity, hidden_width)
    returned = lax.all_to_all(
        lax.all_to_all(owner_terms, "vocab", split_axis=0, concat_axis=0, tiled=True),
        "docs",
        split_axis=1,
        concat_axis=1,
        tiled=True,
    )
    returned = returned.reshape(-1, hidden_width)
    own_rows = returned[slot_index].reshape(docs_here, slot_count, hidden_width).astype(jnp.float32)
    summed = jnp.sum(own_rows, axis=1)
    length_scale = 128.0 * slot_count / doc_len.astype(jnp.float32)
    hidden = jax.nn.softplus(summed * length_scale[:, None] + first_bias).astype(jnp.bfloat16)
    panel_rows = lax.all_gather(head_weight, "docs", axis=1, tiled=True)
    location = jnp.dot(
        hidden,
        lax.all_gather(panel_rows, "vocab", axis=0, tiled=True),
        preferred_element_type=jnp.float32,
    )
    factor_panel = lax.all_gather(factor, "docs", axis=1, tiled=True)
    correlated = lax.dot_general(
        noise_draw,
        lax.all_gather(factor_panel, "vocab", axis=0, tiled=True),
        (((1,), (1,)), ((), ())),
        preferred_element_type=jnp.float32,
    )
    return (location + head_bias + correlated).astype(jnp.bfloat16)


def solution(mesh):
    return jax.shard_map(
        local,
        mesh=mesh,
        in_specs=(
            P(("vocab", "docs"), None, None),
            P(("vocab", "docs"), None),
            P(("vocab", "docs"), None),
            P(("vocab", "docs")),
            P(("vocab", "docs"), None),
            P(),
            P("vocab", "docs"),
            P(),
            P("vocab", "docs"),
            P(("vocab", "docs"), None),
        ),
        out_specs=P(("vocab", "docs"), None),
        check_vma=False,
    )
```

profile of v0, /device:TPU:1, one launch (start us, length us, event | category | flops | bytes accessed | tf_op | source)
XLA Modules:
  0.0 425.2 jit_solution(10619048773508162734)
XLA Ops:
  6.5 50.0 %all_gather.12 = bf16[128,1536]{0,1:T(8,128)(2,1)} all-gather(bf16[128,48]{0,1:T(8,128)(2,1)} %param.16), channel_id=1, replica_groups=mesh['vocab'=16,'docs'=32] {'docs'}, dimensions={1}, use_global_device_ids=true | all-gather | bytes 405504 | tf_op jit(solution)/shard_map/all_gather | solution.py:83
  56.6 0.8 copy.58
  57.4 0.1 eq.46
  57.5 0.1 eq.42
  57.6 0.1 copy.60
  57.7 0.3 fusion.5
  58.1 0.1 broadcast_add_fusion
  58.2 0.3 copy.61
  58.5 0.1 copy.57
  58.6 0.1 mul.48
  58.8 0.1 copy.62
  58.9 0.1 reshape.128
  59.0 0.3 fusion.4
  59.3 3.8 scatter_custom_fusion
  63.1 0.3 reshape.109
  63.3 0.8 copy.63
  64.1 18.7 %all-to-all-start = ((bf16[16,32,2]{1,2,0:T(2,128)(2,1)}), bf16[16,32,2]{1,2,0:T(2,128)(2,1)S(1)}, u32[]{:S(2)}, u32[]{:S(2)}) async-start(bf16[16,32,2]{1,2,0:T(2,128)(2,1)} %copy.63), calls=%async_computation | async-start | bytes 16384 | tf_op jit(solution)/shard_map/all_to_all | solution.py:54
  82.9 2.8 scatter_custom_fusion.1
  85.6 4.3 %all-to-all-done = bf16[16,32,2]{1,2,0:T(2,128)(2,1)S(1)} async-done(((bf16[16,32,2]{1,2,0:T(2,128)(2,1)}), bf16[16,32,2]{1,2,0:T(2,128)(2,1)S(1)}, u32[]{:S(2)}, u32[]{:S(2)}) %all-to-all-start) | async-done | bytes 2080 | tf_op jit(solution)/shard_map/all_to_all | solution.py:54
  90.0 3.9 all-to-all-start.2
  93.9 0.7 copy.64
  94.5 13.3 %all-to-all-done.2 = bf16[16,32,2,128]{3,2,1,0:T(2,128)(2,1)S(1)} async-done(((bf16[16,32,2,128]{3,2,1,0:T(2,128)(2,1)}), bf16[16,32,2,128]{3,2,1,0:T(2,128)(2,1)S(1)}, u32[]{:S(2)}, u32[]{:S(2)}) %all-to-all-start.2) | async-done | bytes 262176 | tf_op jit(solution)/shard_map/all_to_all | solution.py:47
  107.9 4.7 %all-to-all-start.1 = ((bf16[16,32,2]{0,2,1:T(2,128)(2,1)}), bf16[16,32,2]{0,2,1:T(2,128)(2,1)S(1)}, u32[]{:S(2)}, u32[]{:S(2)}) async-start(bf16[16,32,2]{0,2,1:T(2,128)(2,1)} %copy.64), calls=%async_computation.1 | async-start | bytes 32768 | tf_op jit(solution)/shard_map/all_to_all | solution.py:53
  112.6 0.9 copy.67
  113.5 7.7 %all-to-all-done.1 = bf16[16,32,2]{0,2,1:T(2,128)(2,1)S(1)} async-done(((bf16[16,32,2]{0,2,1:T(2,128)(2,1)}), bf16[16,32,2]{0,2,1:T(2,128)(2,1)S(1)}, u32[]{:S(2)}, u32[]{:S(2)}) %all-to-all-start.1) | async-done | bytes 2080 | tf_op jit(solution)/shard_map/all_to_all | solution.py:53
  121.2 4.0 all-to-all-start.3
  125.4 0.2 copy.66
  125.6 0.2 reshape.114
  125.7 0.2 fusion.12
  126.0 8.8 %all-to-all-done.3 = bf16[16,32,2,128]{3,2,0,1:T(2,128)(2,1)S(1)} async-done(((bf16[16,32,2,128]{3,2,0,1:T(2,128)(2,1)}), bf16[16,32,2,128]{3,2,0,1:T(2,128)(2,1)S(1)}, u32[]{:S(2)}, u32[]{:S(2)}) %all-to-all-start.3) | async-done | bytes 262176 | tf_op jit(solution)/shard_map/all_to_all | solution.py:46
  134.8 0.2 copy.68
  135.0 3.5 broadcast_multiply_fusion
  138.5 8.3 %convolution_convert_fusion = bf16[1024,2048]{1,0:T(8,128)(2,1)} fusion(bf16[1024,2048]{1,0:T(8,128)(2,1)} %param.14, bf16[128,8,8,128]{3,2,1,0:T(8,128)(2,1)S(1)} %bitcast.26), kind=kOutput, calls=%fused_computation.3 | convolution fusion | flops 4297064448 | bytes 10485760 | tf_op jit(solution)/shard_map/dot_general | solution.py:67
  146.8 7.6 %reshape.112 = bf16[16,32,2,2048]{3,2,1,0:T(2,128)(2,1)} reshape(bf16[1024,2048]{1,0:T(8,128)(2,1)} %convolution_convert_fusion) | data formatting | bytes 8388608 | tf_op jit(solution)/shard_map/reshape | solution.py:70
  154.4 8.1 %all-to-all-start.4 = ((bf16[16,32,2,2048]{3,2,1,0:T(2,128)(2,1)}), bf16[16,32,2,2048]{3,2,1,0:T(2,128)(2,1)}, u32[]{:S(2)}, u32[]{:S(2)}) async-start(bf16[16,32,2,2048]{3,2,1,0:T(2,128)(2,1)} %reshape.112), calls=%async_computation.4 | async-start | bytes 8388608 | tf_op jit(solution)/shard_map/all_to_all | solution.py:72
  162.5 40.7 %all_gather.14 = bf16[96,1536]{0,1:T(8,128)(2,1)S(1)} all-gather(bf16[96,48]{0,1:T(8,128)(2,1)S(1)} %copy-done.1), channel_id=1, replica_groups=mesh['vocab'=16,'docs'=32] {'docs'}, dimensions={1}, use_global_device_ids=true | all-gather | bytes 304128 | tf_op jit(solution)/shard_map/all_gather | solution.py:89
  203.3 0.9 copy.71
  204.2 65.5 %all-to-all-done.4 = bf16[16,32,2,2048]{3,2,1,0:T(2,128)(2,1)} async-done(((bf16[16,32,2,2048]{3,2,1,0:T(2,128)(2,1)}), bf16[16,32,2,2048]{3,2,1,0:T(2,128)(2,1)}, u32[]{:S(2)}, u32[]{:S(2)}) %all-to-all-start.4) | async-done | bytes 4194336 | tf_op jit(solution)/shard_map/all_to_all | solution.py:72
  269.7 8.8 %copy.69 = bf16[16,32,2,2048]{3,2,0,1:T(2,128)(2,1)} copy(bf16[16,32,2,2048]{3,2,1,0:T(2,128)(2,1)} %all-to-all-done.4) | data formatting | bytes 8388608 | tf_op jit(solution)/shard_map/all_to_all | solution.py:72
  278.5 5.2 %all-to-all-start.5 = ((bf16[16,32,2,2048]{3,2,0,1:T(2,128)(2,1)}), bf16[16,32,2,2048]{3,2,0,1:T(2,128)(2,1)}, u32[]{:S(2)}, u32[]{:S(2)}) async-start(bf16[16,32,2,2048]{3,2,0,1:T(2,128)(2,1)} %copy.69), calls=%async_computation.5 | async-start | bytes 8388608 | tf_op jit(solution)/shard_map/all_to_all | solution.py:71
  283.8 94.4 %all-to-all-done.5 = bf16[16,32,2,2048]{3,2,0,1:T(2,128)(2,1)} async-done(((bf16[16,32,2,2048]{3,2,0,1:T(2,128)(2,1)}), bf16[16,32,2,2048]{3,2,0,1:T(2,128)(2,1)}, u32[]{:S(2)}, u32[]{:S(2)}) %all-to-all-start.5) | async-done | bytes 4194336 | tf_op jit(solution)/shard_map/all_to_all | solution.py:71
  378.2 8.0 %copy.70 = bf16[16,32,2,2048]{3,2,1,0:T(2,128)(2,1)} copy(bf16[16,32,2,2048]{3,2,0,1:T(2,128)(2,1)} %all-to-all-done.5) | data formatting | bytes 8388608 | tf_op jit(solution)/shard_map/all_to_all | solution.py:71
  386.2 7.2 %reshape.113 = bf16[1024,2048]{1,0:T(8,128)(2,1)} reshape(bf16[16,32,2,2048]{3,2,1,0:T(2,128)(2,1)} %copy.70) | data formatting | bytes 8388608 | tf_op jit(solution)/shard_map/reshape | solution.py:78
  393.4 7.1 %gather_fusion = bf16[512,2048]{1,0:T(8,128)(2,1)S(1)} fusion(bf16[1024,2048]{1,0:T(8,128)(2,1)} %reshape.113, s32[1024]{0:T(1024)S(1)} %pad_clamp_fusion), kind=kCustom, calls=%fused_computation | custom fusion | bytes 4196352 | tf_op jit(solution)/shard_map/gather | solution.py:79
  400.6 3.0 reshape.115
  403.6 4.8 %reduce_sum.19 = f32[128,2048]{1,0:T(8,128)S(1)} reduce(f32[128,4,2048]{2,1,0:T(4,128)} %reshape.115, f32[]{:T(128)} %constant.6.clone.1), dimensions={1}, to_apply=%region_5.6 | reduce | flops 786432 | bytes 5242884 | tf_op jit(solution)/shard_map/reduce_sum | solution.py:80
  408.5 5.1 %convolution_add_fusion.1 = f32[128,1536]{1,0:T(8,128)S(1)} fusion(bf16[2048,1536]{0,1:T(8,128)(2,1)} %all-gather.3.cloned.1.call-done, f32[128,2048]{1,0:T(8,128)S(1)} %reduce_sum.19, f32[2048]{0:T(1024)S(1)} %copy-done.4, f32[128]{0:T(128)S(1)} %convert_divide_fusion, f32[1536]{0:T(1024)S(1)} %copy-done.5), kind=kOutput, calls=%fused_computation.6 | convolution fusion | flops 807862272 | bytes 8141312 | tf_op jit(solution)/shard_map/dot_general | solution.py:84
  413.7 4.7 %fusion = bf16[128,1536]{1,0:T(8,128)(2,1)} fusion(f32[128,1536]{1,0:T(8,128)S(1)} %convolution_add_fusion.1, bf16[128,1536]{1,0:T(8,128)(2,1)S(1)} %copy-done, bf16[1536,1536]{1,0:T(8,128)(2,1)} %all-gather.5.cloned.1.call-done), kind=kOutput, calls=%fused_computation.7 | convolution fusion | flops 604372992 | bytes 6291456 | tf_op jit(solution)/shard_map/dot_general | solution.py:90
  (32 shorter events, 0.3 us)
Async XLA Ops:
  6.5 407.1 %copy-start = (bf16[128,1536]{1,0:T(8,128)(2,1)S(1)}, bf16[128,1536]{1,0:T(8,128)(2,1)}, u32[]{:S(2)}) copy-start(bf16[128,1536]{1,0:T(8,128)(2,1)} %param.19) | copy-start | bytes 1179652
  6.5 52.0 %copy-start.2 = (s32[128,4]{0,1:T(4,128)S(1)}, s32[128,4]{0,1:T(4,128)}, u32[]{:S(2)}) copy-start(s32[128,4]{0,1:T(4,128)} %param.11) | copy-start | bytes 6148
  6.5 52.2 %copy-start.3 = (s32[128,4]{0,1:T(4,128)S(1)}, s32[128,4]{0,1:T(4,128)}, u32[]{:S(2)}) copy-start(s32[128,4]{0,1:T(4,128)} %param.12) | copy-start | bytes 6148
  6.5 402.0 %all-gather.3.cloned.1.call-start = ((), (), s32[]{:S(2)}) async-start(), calls=%async_computation.6 | async-start | bytes 6684672 | tf_op jit(solution)/shard_map/all_gather | solution.py:86
  64.1 25.8 %all-to-all-start = ((bf16[16,32,2]{1,2,0:T(2,128)(2,1)}), bf16[16,32,2]{1,2,0:T(2,128)(2,1)S(1)}, u32[]{:S(2)}, u32[]{:S(2)}) async-start(bf16[16,32,2]{1,2,0:T(2,128)(2,1)} %copy.63), calls=%async_computation | async-start | bytes 16384 | tf_op jit(solution)/shard_map/all_to_all | solution.py:54
  90.0 17.9 %all-to-all-start.2 = ((bf16[16,32,2,128]{3,2,1,0:T(2,128)(2,1)}), bf16[16,32,2,128]{3,2,1,0:T(2,128)(2,1)S(1)}, u32[]{:S(2)}, u32[]{:S(2)}) async-start(bf16[16,32,2,128]{3,2,1,0:T(2,128)(2,1)} %bitcast.6), calls=%async_computation.2 | async-start | bytes 524288 | tf_op jit(solution)/shard_map/all_to_all | solution.py:47
  107.9 13.3 %all-to-all-start.1 = ((bf16[16,32,2]{0,2,1:T(2,128)(2,1)}), bf16[16,32,2]{0,2,1:T(2,128)(2,1)S(1)}, u32[]{:S(2)}, u32[]{:S(2)}) async-start(bf16[16,32,2]{0,2,1:T(2,128)(2,1)} %copy.64), calls=%async_computation.1 | async-start | bytes 32768 | tf_op jit(solution)/shard_map/all_to_all | solution.py:53
  121.2 13.5 %all-to-all-start.3 = ((bf16[16,32,2,128]{3,2,0,1:T(2,128)(2,1)}), bf16[16,32,2,128]{3,2,0,1:T(2,128)(2,1)S(1)}, u32[]{:S(2)}, u32[]{:S(2)}) async-start(bf16[16,32,2,128]{3,2,0,1:T(2,128)(2,1)} %copy.67), calls=%async_computation.3 | async-start | bytes 524288 | tf_op jit(solution)/shard_map/all_to_all | solution.py:46
  154.4 8.1 %copy-start.1 = (bf16[96,48]{0,1:T(8,128)(2,1)S(1)}, bf16[96,48]{0,1:T(8,128)(2,1)}, u32[]{:S(2)}) copy-start(bf16[96,48]{0,1:T(8,128)(2,1)} %param.18) | copy-start | bytes 27652
  154.4 115.3 %all-to-all-start.4 = ((bf16[16,32,2,2048]{3,2,1,0:T(2,128)(2,1)}), bf16[16,32,2,2048]{3,2,1,0:T(2,128)(2,1)}, u32[]{:S(2)}, u32[]{:S(2)}) async-start(bf16[16,32,2,2048]{3,2,1,0:T(2,128)(2,1)} %reshape.112), calls=%async_computation.4 | async-start | bytes 8388608 | tf_op jit(solution)/shard_map/all_to_all | solution.py:72
  162.5 251.2 %all-gather.5.cloned.1.call-start = ((), (), s32[]{:S(2)}) async-start(), calls=%async_computation.7 | async-start | bytes 5013504 | tf_op jit(solution)/shard_map/all_gather | solution.py:92
  278.5 5.2 %copy-start.6 = (s32[128]{0:T(128)S(1)}, s32[128]{0:T(128)}, u32[]{:S(2)}) copy-start(s32[128]{0:T(128)} %param.13) | copy-start | bytes 1540
  278.5 99.7 %all-to-all-start.5 = ((bf16[16,32,2,2048]{3,2,0,1:T(2,128)(2,1)}), bf16[16,32,2,2048]{3,2,0,1:T(2,128)(2,1)}, u32[]{:S(2)}, u32[]{:S(2)}) async-start(bf16[16,32,2,2048]{3,2,0,1:T(2,128)(2,1)} %copy.69), calls=%async_computation.5 | async-start | bytes 8388608 | tf_op jit(solution)/shard_map/all_to_all | solution.py:71
  403.6 4.9 %copy-start.4 = (f32[2048]{0:T(1024)S(1)}, f32[2048]{0:T(1024)}, u32[]{:S(2)}) copy-start(f32[2048]{0:T(1024)} %param.15) | copy-start | bytes 24580
  403.6 4.9 %copy-start.5 = (f32[1536]{0:T(1024)S(1)}, f32[1536]{0:T(1024)}, u32[]{:S(2)}) copy-start(f32[1536]{0:T(1024)} %param.17) | copy-start | bytes 18436
Sparse Core Ops, SparseCore 0:
  56.7 72.7 all-gather.2
  204.3 78.6 all-gather.4
where the time goes:
time: 426 us; the launch traced here: 425 us
  waiting for transfers between devices  194 us (46%)
  blocking collectives  90.8 us (21%)
  local copies, waits for them, and re-layouts  54.5 us (13%)
  starting transfers between devices  44.7 us (10%)
  matrix products  18.1 us (4%)
  between operations  13.7 us (3%)
  other arithmetic  9.24 us (2%)
    all_to_all x1, waiting for transfers between devices, local(): lax.all_to_all(lax.all_to_all(owner_terms, 'vocab', split_axis=0, concat_...  94.4 us
    all_to_all x1, waiting for transfers between devices, local(): lax.all_to_all(owner_terms, 'vocab', split_axis=0, concat_axis=0, tiled=T...  65.5 us
    all_gather x1, blocking collectives, local(): panel_rows = lax.all_gather(head_weight, 'docs', axis=1, tiled=True)  50 us
    all_gather x1, blocking collectives, local(): factor_panel = lax.all_gather(factor, 'docs', axis=1, tiled=True)  40.7 us
    all_to_all x1, starting transfers between devices, local(): lax.all_to_all(send_sub, 'vocab', split_axis=0, concat_axis=0, tiled=True)  18.7 us
    all_to_all x1, waiting for transfers between devices, local(): lax.all_to_all(send_rows, 'vocab', split_axis=0, concat_axis=0, tiled=True)  13.3 us
    all_to_all x1, waiting for transfers between devices, local(): lax.all_to_all(lax.all_to_all(send_rows, 'vocab', split_axis=0, concat_ax...  8.81 us
    all_to_all x1, local copies, waits for them, and re-layouts, local(): lax.all_to_all(owner_terms, 'vocab', split_axis=0, concat_axis=0, tiled=T...  8.8 us
  transfers between devices with their start and end apart: 8, of which 6 were waited for; matrix products, arithmetic and copies ran while one was open for 18% of the time, Pallas kernels for 0%

commit v1 on v0

--- a/solution.py
+++ b/solution.py
@@ -86,7 +86,9 @@
         lax.all_gather(panel_rows, "vocab", axis=0, tiled=True),
         preferred_element_type=jnp.float32,
     )
-    factor_panel = lax.all_gather(factor, "docs", axis=1, tiled=True)
+    factor_panel = jnp.concatenate(
+        lax.all_to_all(jnp.stack([factor] * lax.axis_size("docs")), "docs", 0, 0), axis=1
+    )
     correlated = lax.dot_general(
         noise_draw,
         lax.all_gather(factor_panel, "vocab", axis=0, tiled=True),

time: 426 us -> 446 us (1.047)
  waiting for transfers between devices: 194 us -> 242 us
  blocking collectives: 90.8 us -> 49.2 us
  starting transfers between devices: 44.7 us -> 54.7 us
    all_to_all x1, waiting for transfers between devices: 65.5 us -> 115 us  [local(): lax.all_to_all(owner_terms, 'vocab', split_axis=0, concat_axis=0, tiled=T...]
    all_gather x1 -> x0, blocking collectives: 40.7 us -> none  [local(): factor_panel = lax.all_gather(factor, 'docs', axis=1, tiled=True)]
    all_to_all x0 -> x1, starting transfers between devices: none -> 6.26 us  [local(): lax.all_to_all(jnp.stack([factor] * lax.axis_size('docs')), 'docs', 0, 0)]
    all_to_all x1, starting transfers between devices: 5.22 us -> 9.81 us  [local(): lax.all_to_all(lax.all_to_all(owner_terms, 'vocab', split_axis=0, concat_...]
  transfers between devices with their start and end apart: 8 -> 9, of which waited for: 6 -> 6; matrix products, arithmetic and copies ran while one was open for 18% -> 18% of each run, Pallas kernels for 0% -> 0%
where the time goes in v1:
time: 446 us; the launch traced here: 442 us
  waiting for transfers between devices  242 us (54%)
  local copies, waits for them, and re-layouts  55.2 us (12%)
  starting transfers between devices  54.7 us (12%)
  blocking collectives  49.2 us (11%)
  matrix products  18.1 us (4%)
  between operations  13.7 us (3%)
  other arithmetic  9.24 us (2%)
    all_to_all x1, waiting for transfers between devices, local(): lax.all_to_all(owner_terms, 'vocab', split_axis=0, concat_axis=0, tiled=T...  115 us
    all_to_all x1, waiting for transfers between devices, local(): lax.all_to_all(lax.all_to_all(owner_terms, 'vocab', split_axis=0, concat_...  92.3 us
    all_gather x1, blocking collectives, local(): panel_rows = lax.all_gather(head_weight, 'docs', axis=1, tiled=True)  49.2 us
    all_to_all x1, starting transfers between devices, local(): lax.all_to_all(send_sub, 'vocab', split_axis=0, concat_axis=0, tiled=True)  19.8 us
    all_to_all x1, waiting for transfers between devices, local(): lax.all_to_all(send_rows, 'vocab', split_axis=0, concat_axis=0, tiled=True)  13.4 us
    all_to_all x1, starting transfers between devices, local(): lax.all_to_all(lax.all_to_all(owner_terms, 'vocab', split_axis=0, concat_...  9.81 us
    all_to_all x1, waiting for transfers between devices, local(): lax.all_to_all(lax.all_to_all(send_rows, 'vocab', split_axis=0, concat_ax...  8.99 us
  transfers between devices with their start and end apart: 9, of which 6 were waited for; matrix products, arithmetic and copies ran while one was open for 18% of the time, Pallas kernels for 0%

profile of v1, /device:TPU:1, one launch (start us, length us, event | category | flops | bytes accessed | tf_op | source)
XLA Modules:
  0.0 441.7 jit_solution(930108816104330512)
XLA Ops:
  6.5 49.2 %all_gather.9 = bf16[128,1536]{0,1:T(8,128)(2,1)} all-gather(bf16[128,48]{0,1:T(8,128)(2,1)} %param.16), channel_id=1, replica_groups=mesh['vocab'=16,'docs'=32] {'docs'}, dimensions={1}, use_global_device_ids=true | all-gather | bytes 405504 | tf_op jit(solution)/shard_map/all_gather | solution.py:83
  55.8 0.8 copy.59
  56.5 0.1 eq.46
  56.6 0.1 eq.42
  56.8 0.1 copy.61
  56.9 0.3 fusion.5
  57.3 0.3 copy.62
  57.7 0.1 copy.58
  57.8 0.1 mul.48
  57.9 0.1 copy.63
  58.1 0.1 reshape.138
  58.2 0.3 fusion.4
  58.5 3.8 scatter_custom_fusion
  62.3 0.3 reshape.117
  62.5 0.8 copy.64
  63.3 19.8 %all-to-all-start = ((bf16[16,32,2]{1,2,0:T(2,128)(2,1)}), bf16[16,32,2]{1,2,0:T(2,128)(2,1)S(1)}, u32[]{:S(2)}, u32[]{:S(2)}) async-start(bf16[16,32,2]{1,2,0:T(2,128)(2,1)} %copy.64), calls=%async_computation | async-start | bytes 16384 | tf_op jit(solution)/shard_map/all_to_all | solution.py:54
  83.1 2.8 scatter_custom_fusion.1
  85.9 4.3 all-to-all-done
  90.2 4.0 all-to-all-start.2
  94.2 0.7 copy.65
  94.9 13.4 %all-to-all-done.2 = bf16[16,32,2,128]{3,2,1,0:T(2,128)(2,1)S(1)} async-done(((bf16[16,32,2,128]{3,2,1,0:T(2,128)(2,1)}), bf16[16,32,2,128]{3,2,1,0:T(2,128)(2,1)S(1)}, u32[]{:S(2)}, u32[]{:S(2)}) %all-to-all-start.2) | async-done | bytes 262176 | tf_op jit(solution)/shard_map/all_to_all | solution.py:47
  108.3 4.5 %all-to-all-start.1 = ((bf16[16,32,2]{0,2,1:T(2,128)(2,1)}), bf16[16,32,2]{0,2,1:T(2,128)(2,1)S(1)}, u32[]{:S(2)}, u32[]{:S(2)}) async-start(bf16[16,32,2]{0,2,1:T(2,128)(2,1)} %copy.65), calls=%async_computation.1 | async-start | bytes 32768 | tf_op jit(solution)/shard_map/all_to_all | solution.py:53
  112.8 0.9 copy.68
  113.7 7.8 %all-to-all-done.1 = bf16[16,32,2]{0,2,1:T(2,128)(2,1)S(1)} async-done(((bf16[16,32,2]{0,2,1:T(2,128)(2,1)}), bf16[16,32,2]{0,2,1:T(2,128)(2,1)S(1)}, u32[]{:S(2)}, u32[]{:S(2)}) %all-to-all-start.1) | async-done | bytes 2080 | tf_op jit(solution)/shard_map/all_to_all | solution.py:53
  121.5 3.9 all-to-all-start.3
  125.4 0.2 copy.67
  125.6 0.2 reshape.124
  125.8 0.2 fusion.12
  126.0 9.0 %all-to-all-done.3 = bf16[16,32,2,128]{3,2,0,1:T(2,128)(2,1)S(1)} async-done(((bf16[16,32,2,128]{3,2,0,1:T(2,128)(2,1)}), bf16[16,32,2,128]{3,2,0,1:T(2,128)(2,1)S(1)}, u32[]{:S(2)}, u32[]{:S(2)}) %all-to-all-start.3) | async-done | bytes 262176 | tf_op jit(solution)/shard_map/all_to_all | solution.py:46
  135.0 0.8 stack.2
  135.8 6.3 %all-to-all-start.6 = ((bf16[32,96,48]{1,2,0:T(8,128)(2,1)}), bf16[32,96,48]{1,2,0:T(8,128)(2,1)S(1)}, u32[]{:S(2)}, u32[]{:S(2)}) async-start(bf16[32,96,48]{1,2,0:T(8,128)(2,1)} %stack.2), calls=%async_computation.6 | async-start | bytes 786432 | tf_op jit(solution)/shard_map/all_to_all | solution.py:90
  142.1 0.2 copy.69
  142.3 3.5 broadcast_multiply_fusion
  145.8 8.3 %convolution_convert_fusion = bf16[1024,2048]{1,0:T(8,128)(2,1)} fusion(bf16[1024,2048]{1,0:T(8,128)(2,1)} %param.14, bf16[128,8,8,128]{3,2,1,0:T(8,128)(2,1)S(1)} %bitcast.29), kind=kOutput, calls=%fused_computation.3 | convolution fusion | flops 4297064448 | bytes 10485760 | tf_op jit(solution)/shard_map/dot_general | solution.py:67
  154.1 7.6 %reshape.120 = bf16[16,32,2,2048]{3,2,1,0:T(2,128)(2,1)} reshape(bf16[1024,2048]{1,0:T(8,128)(2,1)} %convolution_convert_fusion) | data formatting | bytes 8388608 | tf_op jit(solution)/shard_map/reshape | solution.py:70
  161.7 6.3 %all-to-all-start.4 = ((bf16[16,32,2,2048]{3,2,1,0:T(2,128)(2,1)}), bf16[16,32,2,2048]{3,2,1,0:T(2,128)(2,1)}, u32[]{:S(2)}, u32[]{:S(2)}) async-start(bf16[16,32,2,2048]{3,2,1,0:T(2,128)(2,1)} %reshape.120), calls=%async_computation.4 | async-start | bytes 8388608 | tf_op jit(solution)/shard_map/all_to_all | solution.py:72
  168.1 0.9 copy.72
  169.0 114.8 %all-to-all-done.4 = bf16[16,32,2,2048]{3,2,1,0:T(2,128)(2,1)} async-done(((bf16[16,32,2,2048]{3,2,1,0:T(2,128)(2,1)}), bf16[16,32,2,2048]{3,2,1,0:T(2,128)(2,1)}, u32[]{:S(2)}, u32[]{:S(2)}) %all-to-all-start.4) | async-done | bytes 4194336 | tf_op jit(solution)/shard_map/all_to_all | solution.py:72
  283.8 8.7 %copy.70 = bf16[16,32,2,2048]{3,2,0,1:T(2,128)(2,1)} copy(bf16[16,32,2,2048]{3,2,1,0:T(2,128)(2,1)} %all-to-all-done.4) | data formatting | bytes 8388608 | tf_op jit(solution)/shard_map/all_to_all | solution.py:72
  292.5 9.8 %all-to-all-start.5 = ((bf16[16,32,2,2048]{3,2,0,1:T(2,128)(2,1)}), bf16[16,32,2,2048]{3,2,0,1:T(2,128)(2,1)}, u32[]{:S(2)}, u32[]{:S(2)}) async-start(bf16[16,32,2,2048]{3,2,0,1:T(2,128)(2,1)} %copy.70), calls=%async_computation.5 | async-start | bytes 8388608 | tf_op jit(solution)/shard_map/all_to_all | solution.py:71
  302.4 92.3 %all-to-all-done.5 = bf16[16,32,2,2048]{3,2,0,1:T(2,128)(2,1)} async-done(((bf16[16,32,2,2048]{3,2,0,1:T(2,128)(2,1)}), bf16[16,32,2,2048]{3,2,0,1:T(2,128)(2,1)}, u32[]{:S(2)}, u32[]{:S(2)}) %all-to-all-start.5) | async-done | bytes 4194336 | tf_op jit(solution)/shard_map/all_to_all | solution.py:71
  394.7 8.0 %copy.71 = bf16[16,32,2,2048]{3,2,1,0:T(2,128)(2,1)} copy(bf16[16,32,2,2048]{3,2,0,1:T(2,128)(2,1)} %all-to-all-done.5) | data formatting | bytes 8388608 | tf_op jit(solution)/shard_map/all_to_all | solution.py:71
  402.8 7.2 %reshape.121 = bf16[1024,2048]{1,0:T(8,128)(2,1)} reshape(bf16[16,32,2,2048]{3,2,1,0:T(2,128)(2,1)} %copy.71) | data formatting | bytes 8388608 | tf_op jit(solution)/shard_map/reshape | solution.py:78
  409.9 7.1 %gather_fusion = bf16[512,2048]{1,0:T(8,128)(2,1)S(1)} fusion(bf16[1024,2048]{1,0:T(8,128)(2,1)} %reshape.121, s32[1024]{0:T(1024)S(1)} %pad_clamp_fusion), kind=kCustom, calls=%fused_computation | custom fusion | bytes 4196352 | tf_op jit(solution)/shard_map/gather | solution.py:79
  417.1 3.0 reshape.125
  420.1 4.8 %reduce_sum.19 = f32[128,2048]{1,0:T(8,128)S(1)} reduce(f32[128,4,2048]{2,1,0:T(4,128)} %reshape.125, f32[]{:T(128)} %constant.6.clone.1), dimensions={1}, to_apply=%region_5.6 | reduce | flops 786432 | bytes 5242884 | tf_op jit(solution)/shard_map/reduce_sum | solution.py:80
  425.0 5.1 %convolution_add_fusion.1 = f32[128,1536]{1,0:T(8,128)S(1)} fusion(bf16[2048,1536]{0,1:T(8,128)(2,1)} %all-gather.3.cloned.1.call-done, f32[128,2048]{1,0:T(8,128)S(1)} %reduce_sum.19, f32[2048]{0:T(1024)S(1)} %copy-done.4, f32[128]{0:T(128)S(1)} %convert_divide_fusion, f32[1536]{0:T(1024)S(1)} %copy-done.5), kind=kOutput, calls=%fused_computation.6 | convolution fusion | flops 807862272 | bytes 8141312 | tf_op jit(solution)/shard_map/dot_general | solution.py:84
  430.1 4.7 %fusion = bf16[128,1536]{1,0:T(8,128)(2,1)} fusion(f32[128,1536]{1,0:T(8,128)S(1)} %convolution_add_fusion.1, bf16[128,1536]{1,0:T(8,128)(2,1)S(1)} %copy-done, bf16[1536,1536]{1,0:T(8,128)(2,1)} %all-gather.5.cloned.1.call-done), kind=kOutput, calls=%fused_computation.7 | convolution fusion | flops 604372992 | bytes 6291456 | tf_op jit(solution)/shard_map/dot_general | solution.py:92
  (34 shorter events, 0.4 us)
Async XLA Ops:
  6.5 423.6 %copy-start = (bf16[128,1536]{1,0:T(8,128)(2,1)S(1)}, bf16[128,1536]{1,0:T(8,128)(2,1)}, u32[]{:S(2)}) copy-start(bf16[128,1536]{1,0:T(8,128)(2,1)} %param.19) | copy-start | bytes 1179652
  6.5 51.1 %copy-start.2 = (s32[128,4]{0,1:T(4,128)S(1)}, s32[128,4]{0,1:T(4,128)}, u32[]{:S(2)}) copy-start(s32[128,4]{0,1:T(4,128)} %param.11) | copy-start | bytes 6148
  6.5 51.4 %copy-start.3 = (s32[128,4]{0,1:T(4,128)S(1)}, s32[128,4]{0,1:T(4,128)}, u32[]{:S(2)}) copy-start(s32[128,4]{0,1:T(4,128)} %param.12) | copy-start | bytes 6148
  6.5 418.4 %all-gather.3.cloned.1.call-start = ((), (), s32[]{:S(2)}) async-start(), calls=%async_computation.7 | async-start | bytes 6684672 | tf_op jit(solution)/shard_map/all_gather | solution.py:86
  57.2 77.8 %copy-start.1 = (bf16[96,48]{0,1:T(8,128)(2,1)S(1)}, bf16[96,48]{0,1:T(8,128)(2,1)}, u32[]{:S(2)}) copy-start(bf16[96,48]{0,1:T(8,128)(2,1)} %param.18) | copy-start | bytes 27652
  63.3 26.9 %all-to-all-start = ((bf16[16,32,2]{1,2,0:T(2,128)(2,1)}), bf16[16,32,2]{1,2,0:T(2,128)(2,1)S(1)}, u32[]{:S(2)}, u32[]{:S(2)}) async-start(bf16[16,32,2]{1,2,0:T(2,128)(2,1)} %copy.64), calls=%async_computation | async-start | bytes 16384 | tf_op jit(solution)/shard_map/all_to_all | solution.py:54
  90.2 18.1 %all-to-all-start.2 = ((bf16[16,32,2,128]{3,2,1,0:T(2,128)(2,1)}), bf16[16,32,2,128]{3,2,1,0:T(2,128)(2,1)S(1)}, u32[]{:S(2)}, u32[]{:S(2)}) async-start(bf16[16,32,2,128]{3,2,1,0:T(2,128)(2,1)} %bitcast.6), calls=%async_computation.2 | async-start | bytes 524288 | tf_op jit(solution)/shard_map/all_to_all | solution.py:47
  108.3 13.2 %all-to-all-start.1 = ((bf16[16,32,2]{0,2,1:T(2,128)(2,1)}), bf16[16,32,2]{0,2,1:T(2,128)(2,1)S(1)}, u32[]{:S(2)}, u32[]{:S(2)}) async-start(bf16[16,32,2]{0,2,1:T(2,128)(2,1)} %copy.65), calls=%async_computation.1 | async-start | bytes 32768 | tf_op jit(solution)/shard_map/all_to_all | solution.py:53
  121.5 13.5 %all-to-all-start.3 = ((bf16[16,32,2,128]{3,2,0,1:T(2,128)(2,1)}), bf16[16,32,2,128]{3,2,0,1:T(2,128)(2,1)S(1)}, u32[]{:S(2)}, u32[]{:S(2)}) async-start(bf16[16,32,2,128]{3,2,0,1:T(2,128)(2,1)} %copy.68), calls=%async_computation.3 | async-start | bytes 524288 | tf_op jit(solution)/shard_map/all_to_all | solution.py:46
  135.8 25.9 %all-to-all-start.6 = ((bf16[32,96,48]{1,2,0:T(8,128)(2,1)}), bf16[32,96,48]{1,2,0:T(8,128)(2,1)S(1)}, u32[]{:S(2)}, u32[]{:S(2)}) async-start(bf16[32,96,48]{1,2,0:T(8,128)(2,1)} %stack.2), calls=%async_computation.6 | async-start | bytes 786432 | tf_op jit(solution)/shard_map/all_to_all | solution.py:90
  161.7 122.1 %all-to-all-start.4 = ((bf16[16,32,2,2048]{3,2,1,0:T(2,128)(2,1)}), bf16[16,32,2,2048]{3,2,1,0:T(2,128)(2,1)}, u32[]{:S(2)}, u32[]{:S(2)}) async-start(bf16[16,32,2,2048]{3,2,1,0:T(2,128)(2,1)} %reshape.120), calls=%async_computation.4 | async-start | bytes 8388608 | tf_op jit(solution)/shard_map/all_to_all | solution.py:72
  168.1 262.1 %all-gather.5.cloned.1.call-start = ((), (), s32[]{:S(2)}) async-start(), calls=%async_computation.8 | async-start | bytes 5013504 | tf_op jit(solution)/shard_map/all_gather | solution.py:94
  292.5 9.8 %copy-start.6 = (s32[128]{0:T(128)S(1)}, s32[128]{0:T(128)}, u32[]{:S(2)}) copy-start(s32[128]{0:T(128)} %param.13) | copy-start | bytes 1540
  292.5 102.2 %all-to-all-start.5 = ((bf16[16,32,2,2048]{3,2,0,1:T(2,128)(2,1)}), bf16[16,32,2,2048]{3,2,0,1:T(2,128)(2,1)}, u32[]{:S(2)}, u32[]{:S(2)}) async-start(bf16[16,32,2,2048]{3,2,0,1:T(2,128)(2,1)} %copy.70), calls=%async_computation.5 | async-start | bytes 8388608 | tf_op jit(solution)/shard_map/all_to_all | solution.py:71
  420.1 4.9 %copy-start.4 = (f32[2048]{0:T(1024)S(1)}, f32[2048]{0:T(1024)}, u32[]{:S(2)}) copy-start(f32[2048]{0:T(1024)} %param.15) | copy-start | bytes 24580
  420.1 4.9 %copy-start.5 = (f32[1536]{0:T(1024)S(1)}, f32[1536]{0:T(1024)}, u32[]{:S(2)}) copy-start(f32[1536]{0:T(1024)} %param.17) | copy-start | bytes 18436
Sparse Core Ops, SparseCore 0:
  55.9 74.2 all-gather.2
  171.0 111.6 all-gather.4
